TPU v7x, 32 devices: a whole 2x2x4 slice. The times are simulated.
32 devices in a mesh: dom: 16 (over z, x, core), feat: 2 (over y).
Axes of the slice: x: 2, y: 2, z: 4, core: 2. Of those that a mesh axis runs over, the one named last changes fastest.
Arguments:
- features: float32 [32768, 512], P('dom', 'feat'), may hold values from -6 to 6
- infill_mask: int32 [32768], P('dom'), may hold values 0 or 1
- mask_token: float32 [512], P('feat'), may hold values from -4 to 4
- local_rows: int32 [16, 64], P('dom'), may hold values from 0 to 15
- local_cols: int32 [16, 64], P('dom'), may hold values from 12 to 35, as said below
- local_tiles: float32 [16, 64, 128, 128], P('dom'), may hold values from -0.1875 to 0.1875
- hub_ids: int32 [512], P('dom'), may hold values from 0 to 32767, as said below
- hub_count: int32 [16], P('dom'), may hold values from 16 to 64, as said below
- hub_rows: int32 [16, 64], P('dom'), may hold values from 0 to 15
- hub_panels: int32 [16, 64], P('dom'), may hold values from 0 to 3
- hub_tiles: float32 [16, 64, 128, 128], P('dom'), may hold values from -0.1875 to 0.1875
- mix_weight: float32 [512, 512], P(None, 'feat'), may hold values from -0.25 to 0.25
- mix_bias: float32 [512], P('feat'), may hold values from -3 to 3
- norm_gain: float32 [512], P('feat'), may hold values from 0.25 to 1.75
Outputs:
- updated: float32 [32768, 512], P('dom', 'feat')
Inputs may be any that keep to these rules, and one draw needn't show every extreme that they name: `hub_ids`: index block k of 32 entries holds distinct vertices of partition k. `hub_count`: some partition has all 64 slots live. `local_cols`: each local tile's column block differs from its row block plus 2048 // 128 by at most 4, and in every partition by exactly 4 on both sides.
All inputs are finite; a program needn't handle non-finite values. No bound on the sum of `infill_mask` on one device may be relied on, other than what follows from the above.
Results may differ from a plain program's by a relative error of at most 0.0003.
Values sent between devices are 32-bit elements; how exact they have to be, the bound alone decides.
A program may use at most 128 MiB of HBM per device.

v0:
```python
import jax
import jax.numpy as jnp
from jax import lax
from jax.sharding import PartitionSpec as P


def with_halo(cells, sides, width):
    for axis, dim in sides:
        count = lax.axis_size(axis)
        ends = count - 1
        head = lax.slice_in_dim(cells, 0, width, axis=dim)
        tail = lax.slice_in_dim(cells, cells.shape[dim] - width, cells.shape[dim], axis=dim)
        cells = jnp.concatenate(
            [
                lax.ppermute(tail, axis, [(i, (i + 1) % count) for i in range(ends)]),
                cells,
                lax.ppermute(head, axis, [((i + 1) % count, i) for i in range(ends)]),
            ],
            axis=dim,
        )
    return cells


def block_sum(row_ids, tiles, picked, blocks, weights):
    highest = lax.Precision.HIGHEST
    products = jnp.einsum("tij,tjf->tif", tiles, picked, precision=highest)
    onehot = (row_ids[None, :] == jnp.arange(blocks, dtype=jnp.int32)[:, None]).astype(
        jnp.float32
    ) * weights[None, :]
    return jnp.einsum("rt,tif->rif", onehot, products, precision=highest)


def shards(
    features,
    infill_mask,
    mask_token,
    local_rows,
    local_cols,
    local_tiles,
    hub_ids,
    hub_count,
    hub_rows,
    hub_panels,
    hub_tiles,
    mix_weight,
    mix_bias,
    norm_gain,
):
    highest = lax.Precision.HIGHEST
    rows = features.shape[0]
    half = features.shape[1]
    blocks = rows // 128
    first_row = lax.axis_index("dom") * rows
    filled = jnp.where(infill_mask[:, None] == 1, mask_token[None, :], features)
    extended = with_halo(filled, (("dom", 0),), rows)
    ext_blocks = extended.reshape(3 * blocks, 128, half)
    col_ids = local_cols[0]
    owned_hubs = filled[hub_ids - first_row]
    every_hub = lax.all_gather(owned_hubs, "dom", axis=0, tiled=True)
    panels = every_hub.reshape(-1, 128, half)
    loc_count = local_rows.shape[1]
    slot_count = hub_rows.shape[1]
    total = block_sum(
        local_rows[0],
        local_tiles[0],
        ext_blocks[col_ids],
        blocks,
        jnp.ones((loc_count,), jnp.float32),
    )
    live = (jnp.arange(slot_count, dtype=jnp.int32) < hub_count[0]).astype(jnp.float32)
    total = total + block_sum(hub_rows[0], hub_tiles[0], panels[hub_panels[0]], blocks, live)
    aggregate = total.reshape(rows, half)
    full_aggregate = lax.all_gather(aggregate, "feat", axis=1, tiled=True)
    pre = jnp.dot(full_aggregate, mix_weight, precision=highest) + mix_bias[None, :]
    hidden = filled + jax.nn.silu(pre)
    sum_one, sum_two = lax.psum((jnp.sum(hidden, 1), jnp.sum(hidden * hidden, 1)), "feat")
    width = half * lax.axis_size("feat")
    mean_val = (sum_one / width)[:, None]
    square_val = (sum_two / width)[:, None]
    scale_val = lax.rsqrt(square_val - mean_val * mean_val + 1e-05)
    return (hidden - mean_val) * scale_val * norm_gain[None, :]


def solution(mesh):
    in_specs = (
        P("dom", "feat"),
        P("dom"),
        P("feat"),
        P("dom", None),
        P("dom", None),
        P("dom", None, None, None),
        P("dom"),
        P("dom"),
        P("dom", None),
        P("dom", None),
        P("dom", None, None, None),
        P(None, "feat"),
        P("feat"),
        P("feat"),
    )
    out_specs = P("dom", "feat")
    return jax.shard_map(shards, mesh=mesh, in_specs=in_specs, out_specs=out_specs, check_vma=False)
```

profile of v0, /device:TPU:0, one launch (start us, length us, event | category | flops | bytes accessed | tf_op | source)
XLA Modules:
  0.0 257.4 jit_solution(2771702725690551776)
XLA Ops:
  6.5 0.0 copy-start
  6.5 0.0 copy-start.1
  6.5 0.0 copy-start.2
  6.5 0.0 copy-start.7
  6.5 0.0 copy-start.8
  6.5 0.0 all-gather.3.cloned.1.call-start
  6.6 2.9 %copy.18 = f32[2048,256]{0,1:T(8,128)} copy(f32[2048,256]{1,0:T(8,128)} %param.14) | data formatting | bytes 4194304 | tf_op args[0]
  9.5 0.0 copy-done.1
  9.5 0.0 copy-done.2
  9.6 1.8 broadcast_select_fusion
  11.4 1.3 collective-permute-start.1
  12.7 4.4 %collective-permute-start = (f32[2048,256]{0,1:T(8,128)S(1)}, f32[2048,256]{0,1:T(8,128)}, u32[]{:S(2)}, u32[]{:S(2)}) collective-permute-start(f32[2048,256]{0,1:T(8,128)S(1)} %broadcast_select_fusion), channel_id=1, source_target_pairs={{0,2},{2,4},{4,6},{6,8},{8,10},{10,12},{12,14},{14,16},{16,18},{18... | collective-permute-start | bytes 6291464 | tf_op jit(solution)/shard_map/ppermute | solution.py:15
  17.0 0.0 copy-done.7
  17.0 0.0 copy-done.8
  17.0 1.8 copy.20
  18.9 2.2 gather_fusion.1
  21.1 54.9 %all-gather = f32[512,256]{1,0:T(8,128)S(1)} all-gather(f32[32,256]{1,0:T(8,128)S(1)} %gather_fusion.1), channel_id=2, replica_groups=mesh['dom'=16,'feat'=2] {'dom'}, dimensions={0}, use_global_device_ids=true | all-gather | bytes 557056 | tf_op jit(solution)/shard_map/all_gather | solution.py:59
  76.0 4.3 %gather_fusion.2 = f32[64,128,256]{2,1,0:T(8,128)} fusion(f32[4,128,256]{2,1,0:T(8,128)S(1)} %bitcast.39, s32[1024]{0:T(1024)S(1)} %pad_clamp_fusion), kind=kCustom, calls=%fused_computation.2 | custom fusion | bytes 16777472 | tf_op jit(solution)/shard_map/gather | solution.py:71
  80.3 19.6 %fusion.4 = f32[64,256,128]{2,1,0:T(8,128)} fusion(f32[64,128,256]{2,1,0:T(8,128)} %gather_fusion.2, f32[1,64,128,128]{3,2,1,0:T(8,128)} %param.24), kind=kOutput, calls=%fused_computation.8 | convolution fusion | flops 3221225472 | bytes 20971520 | tf_op jit(solution)/shard_map/tij,tjf->tif/dot_general | solution.py:26
  99.9 0.0 copy-start.9
  99.9 0.0 copy-start.4
  99.9 9.2 %copy.24 = f32[64,256,128]{1,0,2:T(8,128)} copy(f32[64,256,128]{2,1,0:T(8,128)} %fusion.4) | data formatting | bytes 16777216 | tf_op jit(solution)/shard_map/tij,tjf->tif/dot_general | solution.py:26
  109.8 0.0 copy-done.9
  109.8 0.0 copy-done.4
  109.8 7.3 %fusion = f32[16,128,256]{2,0,1:T(8,128)} fusion(f32[64,256,128]{1,0,2:T(8,128)} %copy.24, f32[64]{0:T(128)S(1)} %compare_convert_fusion, s32[64]{0:T(128)S(1)} %bitcast.42), kind=kOutput, calls=%fused_computation.3 | convolution fusion | flops 402655232 | bytes 10486272 | tf_op jit(solution)/shard_map/rt,tif->rif/dot_general | solution.py:30
  117.1 0.0 collective-permute-done.1
  117.2 0.0 collective-permute-done
  117.2 5.5 %pad_maximum_fusion = f32[6144,256]{0,1:T(8,128)} fusion(f32[2048,256]{0,1:T(8,128)} %collective-permute-done.1, f32[2048,256]{0,1:T(8,128)S(1)} %broadcast_select_fusion, f32[2048,256]{0,1:T(8,128)} %collective-permute-done), kind=kLoop, calls=%fused_computation.7 | loop fusion | flops 3145728 | bytes 12582912 | tf_op jit(solution)/shard_map/concatenate | solution.py:13
  122.6 6.6 %copy.25 = f32[6144,256]{1,0:T(8,128)} copy(f32[6144,256]{0,1:T(8,128)} %pad_maximum_fusion) | data formatting | bytes 12582912 | tf_op jit(solution)/shard_map/reshape | solution.py:56
  129.3 7.1 %gather_fusion = f32[64,128,256]{2,1,0:T(8,128)} fusion(f32[48,128,256]{2,1,0:T(8,128)} %bitcast.40, s32[1024]{0:T(1024)S(1)} %pad_clamp_fusion.2), kind=kCustom, calls=%fused_computation | custom fusion | bytes 16777472 | tf_op jit(solution)/shard_map/gather | solution.py:66
  136.4 19.6 %fusion.6 = f32[64,256,128]{2,1,0:T(8,128)} fusion(f32[64,128,256]{2,1,0:T(8,128)} %gather_fusion, f32[1,64,128,128]{3,2,1,0:T(8,128)} %param.19), kind=kOutput, calls=%fused_computation.10 | convolution fusion | flops 3221225472 | bytes 20971520 | tf_op jit(solution)/shard_map/tij,tjf->tif/dot_general | solution.py:26
  155.9 0.0 copy-start.5
  155.9 9.2 %copy.23 = f32[64,256,128]{1,0,2:T(8,128)} copy(f32[64,256,128]{2,1,0:T(8,128)} %fusion.6) | data formatting | bytes 16777216 | tf_op jit(solution)/shard_map/tij,tjf->tif/dot_general | solution.py:26
  165.1 0.0 copy-done.5
  165.1 7.0 %fusion.8 = f32[16,128,256]{2,0,1:T(8,128)S(1)} fusion(f32[16,128,256]{2,0,1:T(8,128)} %fusion, f32[64,256,128]{1,0,2:T(8,128)} %copy.23, s32[64]{0:T(128)S(1)} %bitcast.43), kind=kOutput, calls=%fused_computation.16 | convolution fusion | flops 403178496 | bytes 12583168 | tf_op jit(solution)/shard_map/rt,tif->rif/dot_general | solution.py:30
  172.1 0.0 copy-start.6
  172.1 2.5 copy.21
  174.7 0.0 all-gather.3.cloned.1.call-update
  174.7 0.0 copy-start.3
  174.7 57.3 %all-gather.3.cloned.1.call-done = f32[2048,512]{1,0:T(8,128)} async-done(((f32[2048,256]{1,0:T(8,128)}), f32[2048,512]{1,0:T(8,128)}) %all-gather.3.cloned.1.call-update) | async-done | bytes 4194320 | tf_op jit(solution)/shard_map/all_gather | solution.py:73
  232.0 0.0 copy-done
  232.0 0.0 copy-done.6
  232.0 7.9 %fusion.22 = (f32[2048]{0:T(1024)S(1)}, f32[2048]{0:T(1024)S(1)}, f32[2048,256]{0,1:T(8,128)}) fusion(f32[2048,256]{0,1:T(8,128)S(1)} %broadcast_select_fusion, f32[256]{0:T(256)S(1)} %copy-done.6, f32[2048,512]{1,0:T(8,128)} %all-gather.3.cloned.1.call-done, f32[512,256]{1,0:T(8,128)S(1)} %copy-done), kind=kOutput, calls=%fused_computation.40 | convolution fusion | flops 3225939968 | bytes 8930304 | tf_op jit(solution)/shard_map/dot_general | solution.py:74
  239.9 6.9 %all-reduce = (f32[2048]{0:T(1024)S(1)}, f32[2048]{0:T(1024)S(1)}) all-reduce(f32[2048]{0:T(1024)S(1)} %get-tuple-element.6, f32[2048]{0:T(1024)S(1)} %get-tuple-element.5), channel_id=1, replica_groups=mesh['dom'=16,'feat'=2] {'feat'}, use_global_device_ids=true, to_apply=%region_3.4 | all-reduce | flops 4096 | bytes 32768 | tf_op jit(solution)/shard_map/psum | solution.py:76
  246.9 0.0 copy-done.3
  246.9 1.9 multiply_multiply_fusion
  248.7 1.8 copy.22
  (9 shorter events, 0.1 us)
Async XLA Ops:
  6.5 225.5 %copy-start = (f32[512,256]{1,0:T(8,128)S(1)}, f32[512,256]{1,0:T(8,128)}, u32[]{:S(2)}) copy-start(f32[512,256]{1,0:T(8,128)} %param.25) | copy-start | bytes 1572868
  6.5 3.0 %copy-start.1 = (s32[2048]{0:T(1024)S(1)}, s32[2048]{0:T(1024)}, u32[]{:S(2)}) copy-start(s32[2048]{0:T(1024)} %param.15) | copy-start | bytes 24580
  6.5 3.0 %copy-start.2 = (f32[256]{0:T(256)S(1)}, f32[256]{0:T(256)}, u32[]{:S(2)}) copy-start(f32[256]{0:T(256)} %param.16) | copy-start | bytes 3076
  6.5 10.5 %copy-start.7 = (s32[1,64]{1,0:T(1,128)S(1)}, s32[1,64]{1,0:T(1,128)}, u32[]{:S(2)}) copy-start(s32[1,64]{1,0:T(1,128)} %param.23) | copy-start | bytes 772
  6.5 10.5 %copy-start.8 = (s32[32]{0:T(128)S(1)}, s32[32]{0:T(128)}, u32[]{:S(2)}) copy-start(s32[32]{0:T(128)} %param.20) | copy-start | bytes 388
  6.5 225.5 %all-gather.3.cloned.1.call-start = ((), (), s32[]{:S(2)}) async-start(), calls=%async_computation | async-start | bytes 6291456 | tf_op jit(solution)/shard_map/all_gather | solution.py:73
  11.4 105.8 %collective-permute-start.1 = (f32[2048,256]{0,1:T(8,128)S(1)}, f32[2048,256]{0,1:T(8,128)}, u32[]{:S(2)}, u32[]{:S(2)}) collective-permute-start(f32[2048,256]{0,1:T(8,128)S(1)} %broadcast_select_fusion), channel_id=1, source_target_pairs={{2,0},{4,2},{6,4},{8,6},{10,8},{12,10},{14,12},{16,14},{18,16},{20... | collective-permute-start | bytes 6291464 | tf_op jit(solution)/shard_map/ppermute | solution.py:17
  12.7 104.5 %collective-permute-start = (f32[2048,256]{0,1:T(8,128)S(1)}, f32[2048,256]{0,1:T(8,128)}, u32[]{:S(2)}, u32[]{:S(2)}) collective-permute-start(f32[2048,256]{0,1:T(8,128)S(1)} %broadcast_select_fusion), channel_id=1, source_target_pairs={{0,2},{2,4},{4,6},{6,8},{8,10},{10,12},{12,14},{14,16},{16,18},{18... | collective-permute-start | bytes 6291464 | tf_op jit(solution)/shard_map/ppermute | solution.py:15
  99.9 9.9 %copy-start.9 = (s32[1,64]{1,0:T(1,128)S(1)}, s32[1,64]{1,0:T(1,128)}, u32[]{:S(2)}) copy-start(s32[1,64]{1,0:T(1,128)} %param.18) | copy-start | bytes 772
  99.9 9.9 %copy-start.4 = (s32[1,64]{1,0:T(1,128)S(1)}, s32[1,64]{1,0:T(1,128)}, u32[]{:S(2)}) copy-start(s32[1,64]{1,0:T(1,128)} %param.22) | copy-start | bytes 772
  155.9 9.2 %copy-start.5 = (s32[1,64]{1,0:T(1,128)S(1)}, s32[1,64]{1,0:T(1,128)}, u32[]{:S(2)}) copy-start(s32[1,64]{1,0:T(1,128)} %param.17) | copy-start | bytes 772
  172.1 59.9 %copy-start.6 = (f32[256]{0:T(256)S(1)}, f32[256]{0:T(256)}, u32[]{:S(2)}) copy-start(f32[256]{0:T(256)} %param.26) | copy-start | bytes 3076
  174.7 72.2 %copy-start.3 = (f32[256]{0:T(256)S(1)}, f32[256]{0:T(256)}, u32[]{:S(2)}) copy-start(f32[256]{0:T(256)} %param.27) | copy-start | bytes 3076
Sparse Core Ops, SparseCore 0:
  174.8 57.1 all-gather.2
where the time goes:
time: 258 us; the launch traced here: 257 us
  blocking collectives  61.8 us (24%)
  matrix products  61.4 us (24%)
  waiting for transfers between devices  57.4 us (22%)
  local copies, waits for them, and re-layouts  47.8 us (19%)
  between operations  14.2 us (6%)
  other arithmetic  9.2 us (4%)
  starting transfers between devices  5.68 us (2%)
    all_gather x1, waiting for transfers between devices, shards(): full_aggregate = lax.all_gather(aggregate, 'feat', axis=1, tiled=True)  57.3 us
    all_gather x1, blocking collectives, shards(): every_hub = lax.all_gather(owned_hubs, 'dom', axis=0, tiled=True)  54.9 us
    dot_general x2, matrix products, block_sum(): products = jnp.einsum('tij,tjf->tif', tiles, picked, precision=highest)  39.2 us
    dot_general x2, local copies, waits for them, and re-layouts, block_sum(): products = jnp.einsum('tij,tjf->tif', tiles, picked, precision=highest)  18.4 us
    dot_general x2, matrix products, block_sum(): return jnp.einsum('rt,tif->rif', onehot, products, precision=highest)  14.3 us
    dot_general x1, matrix products, shards(): jnp.dot(full_aggregate, mix_weight, precision=highest) + mix_bias[None, :]  7.89 us
    gather x1, local copies, waits for them, and re-layouts, shards(): ext_blocks[col_ids]  7.09 us
    psum x1, blocking collectives, shards(): lax.psum((jnp.sum(hidden, 1), jnp.sum(hidden * hidden, 1)), 'feat')  6.9 us
  transfers between devices with their start and end apart: 3, of which 1 were waited for; matrix products, arithmetic and copies ran while one was open for 17% of the time, Pallas kernels for 0%

commit v1 on v0

v1 whole, which is shorter than its diff:
```python
import functools

import jax
import jax.numpy as jnp
from jax import lax
from jax.experimental import pallas as pl
from jax.experimental.pallas import tpu as pltpu
from jax.sharding import PartitionSpec as P

REACH = 4
BLK = 128
F32 = jnp.float32
BF16 = jnp.bfloat16


def split(x):
    high = x.astype(BF16)
    low = (x - high.astype(F32)).astype(BF16)
    return high, low


def left_form(x):
    high, low = split(x)
    return jnp.concatenate([high, low, high], axis=1)


def right_form(x):
    high, low = split(x)
    return jnp.concatenate([high, high, low], axis=0)


def kernel(
    n,
    rows,
    half,
    hd,
    slots,
    tiles,
    chunk,
    feat_ref,
    mask_ref,
    token_ref,
    meta_ref,
    ltiles_ref,
    htiles_ref,
    w_ref,
    bias_ref,
    gain_ref,
    out_ref,
    fil,
    halo_lo,
    halo_hi,
    hubs,
    ext_b,
    hub_b,
    tl,
    sums,
    agg,
    other,
    hid,
    w_b,
    st_out,
    st_in,
    tile_sem,
    hub_send,
    hub_recv,
    halo_send,
    halo_recv,
    agg_send,
    agg_recv,
    st_send,
    st_recv,
    out_sem,
):
    blocks = rows // BLK
    panels = n * hd // BLK
    chunks = rows // chunk
    chips = n // 2
    me = lax.axis_index("dom")
    side = lax.axis_index("feat")
    core = lax.rem(me, 2)
    sibling = me + 1 - 2 * core
    halo = REACH * BLK

    barrier = pltpu.get_barrier_semaphore()

    def greet(j, _):
        pl.semaphore_signal(barrier, inc=1, device_id={"dom": lax.rem(me + j, n)})
        return 0

    lax.fori_loop(1, n, greet, 0)
    pl.semaphore_signal(barrier, inc=1, device_id={"feat": 1 - side})

    hub_tiles_copy = pltpu.make_async_copy(htiles_ref, tl.at[pl.ds(0, slots)], tile_sem.at[0])
    loc_tiles_copy = pltpu.make_async_copy(ltiles_ref, tl.at[pl.ds(slots, tiles)], tile_sem.at[1])
    hub_tiles_copy.start()
    loc_tiles_copy.start()

    token = token_ref[...]

    def fill(b, _):
        at = pl.ds(pl.multiple_of(b * BLK, BLK), BLK)
        flags = mask_ref[pl.ds(b, 1), :].astype(F32)
        turned = jnp.broadcast_to(flags, (BLK, BLK)).T
        wide = jnp.concatenate([turned] * (half // BLK), axis=1)
        got = jnp.where(wide == 1.0, jnp.broadcast_to(token, (BLK, half)), feat_ref[at, :])
        fil[at, :] = got
        ext_b[REACH + b] = right_form(got)
        return 0

    lax.fori_loop(0, blocks, fill, 0)

    ids_at = tiles + slots + tiles + slots + blocks
    base = me * hd

    def pick(i, _):
        hubs[pl.ds(base + i, 1), :] = fil[pl.ds(meta_ref[ids_at + i], 1), :]
        return 0

    lax.fori_loop(0, hd, pick, 0)

    pl.semaphore_wait(barrier, n)

    def hub_copy(owner, target, sem_at):
        at = pl.ds(pl.multiple_of(owner * hd, hd), hd)
        return pltpu.make_async_remote_copy(
            src_ref=hubs.at[at],
            dst_ref=hubs.at[at],
            send_sem=hub_send.at[sem_at],
            recv_sem=hub_recv.at[owner],
            device_id={"dom": target},
        )

    def send_far(j, _):
        hub_copy(me, lax.rem(me + 2 * j, n), j).start()
        return 0

    lax.fori_loop(1, chips, send_far, 0)
    hub_copy(me, sibling, 0).start()

    down = pltpu.make_async_remote_copy(
        src_ref=fil.at[pl.ds(0, halo)],
        dst_ref=halo_hi,
        send_sem=halo_send.at[0],
        recv_sem=halo_recv.at[0],
        device_id={"dom": lax.rem(me + n - 1, n)},
    )
    up = pltpu.make_async_remote_copy(
        src_ref=fil.at[pl.ds(rows - halo, halo)],
        dst_ref=halo_lo,
        send_sem=halo_send.at[1],
        recv_sem=halo_recv.at[1],
        device_id={"dom": lax.rem(me + 1, n)},
    )

    @pl.when(me > 0)
    def _():
        down.start()

    @pl.when(me < n - 1)
    def _():
        up.start()

    w_own = w_ref[pl.ds(pl.multiple_of(side * half, half), half), :]
    w_far = w_ref[pl.ds(pl.multiple_of((1 - side) * half, half), half), :]
    w_b[0] = right_form(w_own)
    w_b[1] = right_form(w_far)
    sums[0] = jnp.zeros((BLK, half), F32)

    def forward(j, _):
        owner = lax.rem(me + n - 2 * j, n)
        hub_copy(owner, sibling, 0).wait_recv()
        hub_copy(owner, sibling, chips + j).start()
        return 0

    lax.fori_loop(1, chips, forward, 0)

    def arrive(j, _):
        hub_copy(lax.rem(sibling + n - 2 * j, n), sibling, 0).wait_recv()
        return 0

    lax.fori_loop(0, chips, arrive, 0)

    def panel_form(p, _):
        hub_b[p] = right_form(hubs[pl.ds(pl.multiple_of(p * BLK, BLK), BLK), :])
        return 0

    lax.fori_loop(0, panels, panel_form, 0)
    hub_tiles_copy.wait()

    chain_at = tiles + slots
    group = 4

    def hub_products(g, _):
        for u in range(group):
            t = g * group + u
            got = jnp.dot(left_form(tl[t]), hub_b[meta_ref[tiles + t]], preferred_element_type=F32)
            sums[t + 1] = got + sums[meta_ref[chain_at + t]]
        return 0

    lax.fori_loop(0, slots // group, hub_products, 0)

    @pl.when(me > 0)
    def _():
        up.wait_recv()

    @pl.when(me == 0)
    def _():
        halo_lo[...] = jnp.zeros((halo, half), F32)

    @pl.when(me < n - 1)
    def _():
        down.wait_recv()

    @pl.when(me == n - 1)
    def _():
        halo_hi[...] = jnp.zeros((halo, half), F32)

    for b in range(REACH):
        ext_b[b] = right_form(halo_lo[pl.ds(b * BLK, BLK), :])
        ext_b[REACH + blocks + b] = right_form(halo_hi[pl.ds(b * BLK, BLK), :])
    loc_tiles_copy.wait()

    def loc_products(g, _):
        for u in range(group):
            t = g * group + u
            got = jnp.dot(left_form(tl[slots + t]), ext_b[meta_ref[t]], preferred_element_type=F32)
            sums[slots + t + 1] = got + sums[meta_ref[chain_at + slots + t]]
        return 0

    lax.fori_loop(0, tiles // group, loc_products, 0)

    last_at = chain_at + slots + tiles
    per = chunk // BLK

    def chunk_rows(c):
        return pl.ds(pl.multiple_of(c * chunk, chunk), chunk)

    def agg_copy(c):
        return pltpu.make_async_remote_copy(
            src_ref=agg.at[chunk_rows(c)],
            dst_ref=other.at[chunk_rows(c)],
            send_sem=agg_send.at[c],
            recv_sem=agg_recv.at[c],
            device_id={"feat": 1 - side},
        )

    def st_copy(c):
        return pltpu.make_async_remote_copy(
            src_ref=st_out.at[c],
            dst_ref=st_in.at[c],
            send_sem=st_send.at[c],
            recv_sem=st_recv.at[c],
            device_id={"feat": 1 - side},
        )

    def out_copy(c):
        return pltpu.make_async_copy(hid.at[chunk_rows(c)], out_ref.at[chunk_rows(c)], out_sem.at[c])

    def send_chunk(c, _):
        for u in range(per):
            r = c * per + u
            agg[pl.ds(pl.multiple_of(r * BLK, BLK), BLK), :] = sums[meta_ref[last_at + r]]
        agg_copy(c).start()
        return 0

    lax.fori_loop(0, chunks, send_chunk, 0)

    bias = bias_ref[...]
    gain = gain_ref[...]
    width = 2.0 * half

    def finish(c):
        st_copy(c).wait_recv()
        both = st_out[c] + st_in[c]
        turned = jnp.concatenate([both] * (BLK // 8), axis=0).T
        mean = turned[:, 0:1] / width
        square = turned[:, 4:5] / width
        scale = lax.rsqrt(square - mean * mean + 1e-05)
        hid[chunk_rows(c), :] = (hid[chunk_rows(c), :] - mean) * scale * gain
        out_copy(c).start()

    def mix(c, _):
        at = chunk_rows(c)
        pre = jnp.dot(left_form(agg[at, :]), w_b[0], preferred_element_type=F32)
        agg_copy(c).wait_recv()
        pre = pre + jnp.dot(left_form(other[at, :]), w_b[1], preferred_element_type=F32) + bias
        hidden = fil[at, :] + pre / (1.0 + jnp.exp(-pre))
        hid[at, :] = hidden
        one = jnp.sum(hidden, axis=1, keepdims=True)
        two = jnp.sum(hidden * hidden, axis=1, keepdims=True)
        lane = lax.broadcasted_iota(jnp.int32, (chunk, BLK), 1)
        packed = jnp.where(lax.rem(lane, 8) < 4, jnp.broadcast_to(one, (chunk, BLK)), jnp.broadcast_to(two, (chunk, BLK)))
        st_out[c] = packed.T[0:8, :]
        st_copy(c).start()

        @pl.when(c > 0)
        def _():
            finish(c - 1)

        return 0

    lax.fori_loop(0, chunks, mix, 0)
    finish(chunks - 1)

    def close(c, _):
        agg_copy(c).wait_send()
        st_copy(c).wait_send()
        out_copy(c).wait()
        return 0

    lax.fori_loop(0, chunks, close, 0)

    def close_far(j, _):
        hub_copy(me, sibling, j).wait_send()
        hub_copy(me, sibling, chips + j).wait_send()
        return 0

    lax.fori_loop(1, chips, close_far, 0)
    hub_copy(me, sibling, 0).wait_send()

    @pl.when(me > 0)
    def _():
        down.wait_send()

    @pl.when(me < n - 1)
    def _():
        up.wait_send()


def shards(
    features,
    infill_mask,
    mask_token,
    local_rows,
    local_cols,
    local_tiles,
    hub_ids,
    hub_count,
    hub_rows,
    hub_panels,
    hub_tiles,
    mix_weight,
    mix_bias,
    norm_gain,
):
    rows, half = features.shape
    blocks = rows // BLK
    n = lax.axis_size("dom")
    hd = hub_ids.shape[0]
    tiles = local_rows.shape[1]
    slots = hub_rows.shape[1]
    chunk = 256
    chunks = rows // chunk
    i32 = jnp.int32

    live = jnp.arange(slots, dtype=i32) < hub_count[0]
    row_of = jnp.concatenate([jnp.where(live, hub_rows[0], -1), local_rows[0]])
    total = slots + tiles
    seq = jnp.arange(total, dtype=i32)
    target = jnp.concatenate([row_of, jnp.arange(blocks, dtype=i32)])
    limit = jnp.concatenate([seq, jnp.full((blocks,), total, i32)])
    same = (row_of[None, :] == target[:, None]) & (seq[None, :] < limit[:, None])
    chain = jnp.max(jnp.where(same, seq[None, :] + 1, 0), axis=1)
    meta = jnp.concatenate(
        [
            local_cols[0] - (blocks - REACH),
            hub_panels[0],
            chain,
            hub_ids - lax.axis_index("dom") * rows,
        ]
    )

    vmem = pl.BlockSpec(memory_space=pltpu.VMEM)
    smem = pl.BlockSpec(memory_space=pltpu.SMEM)
    anym = pl.BlockSpec(memory_space=pl.ANY)
    dma = pltpu.SemaphoreType.DMA
    flops = 6 * BLK * BLK * half * total + 6 * rows * 2 * half * half
    return pl.pallas_call(
        functools.partial(kernel, n, rows, half, hd, slots, tiles, chunk),
        out_shape=jax.ShapeDtypeStruct((rows, half), F32),
        in_specs=[vmem, vmem, vmem, smem, anym, anym, vmem, vmem, vmem],
        out_specs=anym,
        scratch_shapes=[
            pltpu.VMEM((rows, half), F32),
            pltpu.VMEM((REACH * BLK, half), F32),
            pltpu.VMEM((REACH * BLK, half), F32),
            pltpu.VMEM((n * hd, half), F32),
            pltpu.VMEM((blocks + 2 * REACH, 3 * BLK, half), BF16),
            pltpu.VMEM((n * hd // BLK, 3 * BLK, half), BF16),
            pltpu.VMEM((total, BLK, BLK), F32),
            pltpu.VMEM((total + 1, BLK, half), F32),
            pltpu.VMEM((rows, half), F32),
            pltpu.VMEM((rows, half), F32),
            pltpu.VMEM((rows, half), F32),
            pltpu.VMEM((2, 3 * half, half), BF16),
            pltpu.VMEM((chunks, 8, chunk), F32),
            pltpu.VMEM((chunks, 8, chunk), F32),
            dma((2,)),
            dma((n,)),
            dma((n,)),
            dma((2,)),
            dma((2,)),
            dma((chunks,)),
            dma((chunks,)),
            dma((chunks,)),
            dma((chunks,)),
            dma((chunks,)),
        ],
        compiler_params=pltpu.CompilerParams(
            collective_id=0, has_side_effects=True, vmem_limit_bytes=58 * 1024 * 1024
        ),
        cost_estimate=pl.CostEstimate(flops=flops, bytes_accessed=13 << 20, transcendentals=rows * half),
    )(
        features,
        infill_mask.reshape(blocks, BLK),
        mask_token[None, :],
        meta,
        local_tiles[0],
        hub_tiles[0],
        mix_weight,
        mix_bias[None, :],
        norm_gain[None, :],
    )


def solution(mesh):
    in_specs = (
        P("dom", "feat"),
        P("dom"),
        P("feat"),
        P("dom", None),
        P("dom", None),
        P("dom", None, None, None),
        P("dom"),
        P("dom"),
        P("dom", None),
        P("dom", None),
        P("dom", None, None, None),
        P(None, "feat"),
        P("feat"),
        P("feat"),
    )
    out_specs = P("dom", "feat")
    return jax.shard_map(shards, mesh=mesh, in_specs=in_specs, out_specs=out_specs, check_vma=False)
```

time: 258 us -> 94.3 us (0.37)
  Pallas kernels: 0 us -> 84.5 us
  blocking collectives: 61.8 us -> 0 us
  matrix products: 61.4 us -> 0 us
  waiting for transfers between devices: 57.4 us -> 0 us
  local copies, waits for them, and re-layouts: 47.8 us -> 3.05 us
  between operations: 14.2 us -> 0.67 us
  starting transfers between devices: 5.68 us -> 0 us
  other arithmetic: 9.2 us -> 5.61 us
    pallas_call x0 -> x1, Pallas kernels: none -> 84.5 us  [shards(): pl.pallas_call(functools.partial(kernel, n, rows, half, hd, slots, tiles,...]
    dot_general x5 -> x0, matrix products: 61.4 us -> none  [the longest x2 39.2 us: block_sum(): products = jnp.einsum('tij,tjf->tif', tiles, picked, precision=highest)]
    all_gather x1 -> x0, waiting for transfers between devices: 57.3 us -> none  [shards(): full_aggregate = lax.all_gather(aggregate, 'feat', axis=1, tiled=True)]
    all_gather x1 -> x0, blocking collectives: 54.9 us -> none  [shards(): every_hub = lax.all_gather(owned_hubs, 'dom', axis=0, tiled=True)]
    dot_general x2 -> x0, local copies, waits for them, and re-layouts: 18.4 us -> none  [block_sum(): products = jnp.einsum('tij,tjf->tif', tiles, picked, precision=highest)]
    gather x3 -> x0, local copies, waits for them, and re-layouts: 13.6 us -> none  [the longest x1 7.09 us: shards(): ext_blocks[col_ids]]
    psum x1 -> x0, blocking collectives: 6.9 us -> none  [shards(): lax.psum((jnp.sum(hidden, 1), jnp.sum(hidden * hidden, 1)), 'feat')]
    reshape x1 -> x0, local copies, waits for them, and re-layouts: 6.63 us -> none  [shards(): ext_blocks = extended.reshape(3 * blocks, 128, half)]
  transfers between devices with their start and end apart: 3 -> 0, of which waited for: 1 -> 0; matrix products, arithmetic and copies ran while one was open for 17% -> 0% of each run, Pallas kernels for 0% -> 0%
where the time goes in v1:
time: 94.3 us; the launch traced here: 93.8 us
  Pallas kernels  84.5 us (90%)
  other arithmetic  5.61 us (6%)
  local copies, waits for them, and re-layouts  3.05 us (3%)
    pallas_call x1, Pallas kernels, shards(): pl.pallas_call(functools.partial(kernel, n, rows, half, hd, slots, tiles,...  84.5 us
    unnamed x1, local copies, waits for them, and re-layouts  3.05 us

profile of v1, /device:TPU:0, one launch (start us, length us, event | category | flops | bytes accessed | tf_op | source)
XLA Modules:
  0.0 93.8 jit_solution(3639967662016061912)
XLA Ops:
  0.7 0.7 compare_select_fusion
  1.3 0.7 broadcast_subtract_fusion
  2.0 0.7 add_bitcast_fusion
  2.6 0.7 pad_add_fusion.1
  3.4 0.7 pad_add_fusion.2
  4.1 0.9 select_reduce_fusion
  5.0 1.3 %pad_add_fusion.meta_ref = s32[304]{0:T(512)} fusion(s32[32]{0:T(128)S(1)} %broadcast_subtract_fusion, s32[144]{0:T(256)S(1)} %select_reduce_fusion, s32[64]{0:T(128)} %bitcast.16, s32[64]{0:T(128)S(1)} %add_bitcast_fusion), kind=kLoop, calls=%fused_computation.3 | loop fusion | flops 912 | bytes 2432 | tf_op jit(solution)/shard_map/concatenate | solution.py:365
  6.3 84.5 %shard_map.136 = f32[2048,256]{1,0:T(8,128)} custom-call(f32[2048,256]{1,0:T(8,128)} %feat_ref.1, s32[16,128]{1,0:T(8,128)} %bitcast.19, f32[1,256]{1,0:T(1,128)} %bitcast.20, s32[304]{0:T(512)} %pad_add_fusion.meta_ref, f32[64,128,128]{2,1,0:T(8,128)} %bitcast.17, f32[64,128,128]{2,1,0:T(8,128)} %bitcast.18, f32[512,256]{1,0:T(8,128)} %w_ref.1, ...), custom_call_target="tpu_custom_call" | custom-call | flops 4831838208 | bytes 13631488 | tf_op jit(solution)/shard_map/pallas_call | solution.py:379
  90.8 3.0 %copy.17 = f32[2048,256]{1,0:T(8,128)} copy(f32[2048,256]{1,0:T(8,128)} %shard_map.136) | data formatting | bytes 4194304
  (1 shorter events, 0.0 us)

commit v2 on v1

--- a/solution.py
+++ b/solution.py
@@ -40,28 +40,42 @@
     feat_ref,
     mask_ref,
     token_ref,
-    meta_ref,
+    cols_ref,
+    panels_ref,
+    ids_ref,
+    chain_ref,
     ltiles_ref,
     htiles_ref,
     w_ref,
     bias_ref,
-    gain_ref,
     out_ref,
     fil,
     halo_lo,
     halo_hi,
+    early,
+    early_in,
+    early_lo,
+    early_hi,
+    hub_out,
+    hub_in,
     hubs,
     ext_b,
     hub_b,
     tl,
     sums,
     agg,
-    other,
+    late,
+    late_in,
     hid,
     w_b,
     st_out,
     st_in,
     tile_sem,
+    feat_sem,
+    early_send,
+    early_recv,
+    hop_send,
+    hop_recv,
     hub_send,
     hub_recv,
     halo_send,
@@ -81,6 +95,16 @@
     core = lax.rem(me, 2)
     sibling = me + 1 - 2 * core
     halo = REACH * BLK
+    part = half // 2
+    pieces = rows // halo
+    mate = {"feat": 1 - side}
+
+    feat_copies = [
+        pltpu.make_async_copy(feat_ref.at[pl.ds(q * halo, halo)], fil.at[pl.ds(q * halo, halo)], feat_sem.at[q])
+        for q in range(pieces)
+    ]
+    for copy in feat_copies:
+        copy.start()
 
     barrier = pltpu.get_barrier_semaphore()
 
@@ -103,23 +127,51 @@
         flags = mask_ref[pl.ds(b, 1), :].astype(F32)
         turned = jnp.broadcast_to(flags, (BLK, BLK)).T
         wide = jnp.concatenate([turned] * (half // BLK), axis=1)
-        got = jnp.where(wide == 1.0, jnp.broadcast_to(token, (BLK, half)), feat_ref[at, :])
+        got = jnp.where(wide == 1.0, jnp.broadcast_to(token, (BLK, half)), fil[at, :])
         fil[at, :] = got
+        early[at, :] = got[:, part:]
         ext_b[REACH + b] = right_form(got)
         return 0
 
-    lax.fori_loop(0, blocks, fill, 0)
-
-    ids_at = tiles + slots + tiles + slots + blocks
-    base = me * hd
+    for q in range(pieces):
+        feat_copies[q].wait()
+        lax.fori_loop(q * REACH, (q + 1) * REACH, fill, 0)
+
+    base = pl.multiple_of(me * hd, hd)
+    first = me * rows
 
     def pick(i, _):
-        hubs[pl.ds(base + i, 1), :] = fil[pl.ds(meta_ref[ids_at + i], 1), :]
+        got = fil[pl.ds(jnp.maximum(ids_ref[i] - first, 0), 1), :]
+        hubs[pl.ds(base + i, 1), 0:half] = got
+        hub_out[pl.ds(i, 1), :] = got[:, part:]
         return 0
 
     lax.fori_loop(0, hd, pick, 0)
 
     pl.semaphore_wait(barrier, n)
+
+    hop = pltpu.make_async_remote_copy(
+        src_ref=hub_out,
+        dst_ref=hub_in,
+        send_sem=hop_send.at[0],
+        recv_sem=hop_recv.at[0],
+        device_id=mate,
+    )
+    hop.start()
+
+    def early_copy(q):
+        at = pl.ds(q * halo, halo)
+        return pltpu.make_async_remote_copy(
+            src_ref=early.at[at],
+            dst_ref=early_in.at[at],
+            send_sem=early_send.at[q],
+            recv_sem=early_recv.at[q],
+            device_id=mate,
+        )
+
+    order = [0, pieces - 1] + list(range(1, pieces - 1))
+    for q in order:
+        early_copy(q).start()
 
     def hub_copy(owner, target, sem_at):
         at = pl.ds(pl.multiple_of(owner * hd, hd), hd)
@@ -130,6 +182,9 @@
             recv_sem=hub_recv.at[owner],
             device_id={"dom": target},
         )
+
+    hop.wait_recv()
+    hubs[pl.ds(base, hd), half:] = hub_in[...]
 
     def send_far(j, _):
         hub_copy(me, lax.rem(me + 2 * j, n), j).start()
@@ -161,10 +216,26 @@
     def _():
         up.start()
 
+    early_down = pltpu.make_async_remote_copy(
+        src_ref=early_in.at[pl.ds(0, halo)],
+        dst_ref=early_hi,
+        send_sem=halo_send.at[2],
+        recv_sem=halo_recv.at[2],
+        device_id={"dom": lax.rem(me + n - 1, n)},
+    )
+    early_up = pltpu.make_async_remote_copy(
+        src_ref=early_in.at[pl.ds(rows - halo, halo)],
+        dst_ref=early_lo,
+        send_sem=halo_send.at[3],
+        recv_sem=halo_recv.at[3],
+        device_id={"dom": lax.rem(me + 1, n)},
+    )
+
     w_own = w_ref[pl.ds(pl.multiple_of(side * half, half), half), :]
     w_far = w_ref[pl.ds(pl.multiple_of((1 - side) * half, half), half), :]
-    w_b[0] = right_form(w_own)
-    w_b[1] = right_form(w_far)
+    w_b[pl.ds(0, 3 * half), :] = right_form(w_own)
+    w_b[pl.ds(3 * half, 3 * part), :] = right_form(w_far[part:, :])
+    w_b[pl.ds(3 * half + 3 * part, 3 * part), :] = right_form(w_far[:part, :])
     sums[0] = jnp.zeros((BLK, half), F32)
 
     def forward(j, _):
@@ -182,23 +253,35 @@
     lax.fori_loop(0, chips, arrive, 0)
 
     def panel_form(p, _):
-        hub_b[p] = right_form(hubs[pl.ds(pl.multiple_of(p * BLK, BLK), BLK), :])
+        hub_b[p] = right_form(hubs[pl.ds(pl.multiple_of(p * BLK, BLK), BLK), 0:half])
         return 0
 
     lax.fori_loop(0, panels, panel_form, 0)
     hub_tiles_copy.wait()
 
-    chain_at = tiles + slots
+    last_at = slots + tiles
+    shift = blocks - REACH
     group = 4
 
     def hub_products(g, _):
         for u in range(group):
             t = g * group + u
-            got = jnp.dot(left_form(tl[t]), hub_b[meta_ref[tiles + t]], preferred_element_type=F32)
-            sums[t + 1] = got + sums[meta_ref[chain_at + t]]
+            got = jnp.dot(left_form(tl[t]), hub_b[panels_ref[0, t]], preferred_element_type=F32)
+            sums[t + 1] = got + sums[chain_ref[t]]
         return 0
 
     lax.fori_loop(0, slots // group, hub_products, 0)
+
+    early_copy(0).wait_recv()
+    early_copy(pieces - 1).wait_recv()
+
+    @pl.when(me > 0)
+    def _():
+        early_down.start()
+
+    @pl.when(me < n - 1)
+    def _():
+        early_up.start()
 
     @pl.when(me > 0)
     def _():
@@ -224,13 +307,12 @@
     def loc_products(g, _):
         for u in range(group):
             t = g * group + u
-            got = jnp.dot(left_form(tl[slots + t]), ext_b[meta_ref[t]], preferred_element_type=F32)
-            sums[slots + t + 1] = got + sums[meta_ref[chain_at + slots + t]]
+            got = jnp.dot(left_form(tl[slots + t]), ext_b[jnp.maximum(cols_ref[0, t] - shift, 0)], preferred_element_type=F32)
+            sums[slots + t + 1] = got + sums[chain_ref[slots + t]]
         return 0
 
     lax.fori_loop(0, tiles // group, loc_products, 0)
 
-    last_at = chain_at + slots + tiles
     per = chunk // BLK
 
     def chunk_rows(c):
@@ -238,11 +320,11 @@
 
     def agg_copy(c):
         return pltpu.make_async_remote_copy(
-            src_ref=agg.at[chunk_rows(c)],
-            dst_ref=other.at[chunk_rows(c)],
+            src_ref=late.at[chunk_rows(c)],
+            dst_ref=late_in.at[chunk_rows(c)],
             send_sem=agg_send.at[c],
             recv_sem=agg_recv.at[c],
-            device_id={"feat": 1 - side},
+            device_id=mate,
         )
 
     def st_copy(c):
@@ -251,7 +333,7 @@
             dst_ref=st_in.at[c],
             send_sem=st_send.at[c],
             recv_sem=st_recv.at[c],
-            device_id={"feat": 1 - side},
+            device_id=mate,
         )
 
     def out_copy(c):
@@ -260,14 +342,71 @@
     def send_chunk(c, _):
         for u in range(per):
             r = c * per + u
-            agg[pl.ds(pl.multiple_of(r * BLK, BLK), BLK), :] = sums[meta_ref[last_at + r]]
+            at = pl.ds(pl.multiple_of(r * BLK, BLK), BLK)
+            got = sums[chain_ref[last_at + r]]
+            agg[at, :] = got
+            late[at, :] = got[:, :part]
         agg_copy(c).start()
         return 0
 
     lax.fori_loop(0, chunks, send_chunk, 0)
 
+    def hub_early(p, _):
+        hub_b[p, :, 0:part] = right_form(hubs[pl.ds(pl.multiple_of(p * BLK, BLK), BLK), half:])
+        return 0
+
+    lax.fori_loop(0, panels, hub_early, 0)
+
+    def hub_products_early(g, _):
+        for u in range(group):
+            t = g * group + u
+            right = hub_b[panels_ref[0, t], :, 0:part]
+            got = jnp.dot(left_form(tl[t]), right, preferred_element_type=F32)
+            sums[t + 1, :, 0:part] = got + sums[chain_ref[t], :, 0:part]
+        return 0
+
+    lax.fori_loop(0, slots // group, hub_products_early, 0)
+
+    for q in range(1, pieces - 1):
+        early_copy(q).wait_recv()
+
+    def own_early(b, _):
+        ext_b[REACH + b, :, 0:part] = right_form(early_in[pl.ds(pl.multiple_of(b * BLK, BLK), BLK), :])
+        return 0
+
+    lax.fori_loop(0, blocks, own_early, 0)
+
+    @pl.when(me > 0)
+    def _():
+        early_up.wait_recv()
+
+    @pl.when(me == 0)
+    def _():
+        early_lo[...] = jnp.zeros((halo, part), F32)
+
+    @pl.when(me < n - 1)
+    def _():
+        early_down.wait_recv()
+
+    @pl.when(me == n - 1)
+    def _():
+        early_hi[...] = jnp.zeros((halo, part), F32)
+
+    for b in range(REACH):
+        ext_b[b, :, 0:part] = right_form(early_lo[pl.ds(b * BLK, BLK), :])
+        ext_b[REACH + blocks + b, :, 0:part] = right_form(early_hi[pl.ds(b * BLK, BLK), :])
+
+    def loc_products_early(g, _):
+        for u in range(group):
+            t = g * group + u
+            right = ext_b[jnp.maximum(cols_ref[0, t] - shift, 0), :, 0:part]
+            got = jnp.dot(left_form(tl[slots + t]), right, preferred_element_type=F32)
+            sums[slots + t + 1, :, 0:part] = got + sums[chain_ref[slots + t], :, 0:part]
+        return 0
+
+    lax.fori_loop(0, tiles // group, loc_products_early, 0)
+
     bias = bias_ref[...]
-    gain = gain_ref[...]
     width = 2.0 * half
 
     def finish(c):
@@ -277,14 +416,17 @@
         mean = turned[:, 0:1] / width
         square = turned[:, 4:5] / width
         scale = lax.rsqrt(square - mean * mean + 1e-05)
-        hid[chunk_rows(c), :] = (hid[chunk_rows(c), :] - mean) * scale * gain
+        hid[chunk_rows(c), :] = (hid[chunk_rows(c), :] - mean) * scale
         out_copy(c).start()
 
     def mix(c, _):
         at = chunk_rows(c)
-        pre = jnp.dot(left_form(agg[at, :]), w_b[0], preferred_element_type=F32)
+        got = jnp.concatenate([sums[chain_ref[last_at + c * per + u], :, 0:part] for u in range(per)], axis=0)
+        left = jnp.concatenate([left_form(agg[at, :]), left_form(got)], axis=1)
+        pre = jnp.dot(left, w_b[pl.ds(0, 3 * half + 3 * part), :], preferred_element_type=F32) + bias
         agg_copy(c).wait_recv()
-        pre = pre + jnp.dot(left_form(other[at, :]), w_b[1], preferred_element_type=F32) + bias
+        right = w_b[pl.ds(3 * half + 3 * part, 3 * part), :]
+        pre = pre + jnp.dot(left_form(late_in[at, :]), right, preferred_element_type=F32)
         hidden = fil[at, :] + pre / (1.0 + jnp.exp(-pre))
         hid[at, :] = hidden
         one = jnp.sum(hidden, axis=1, keepdims=True)
@@ -317,15 +459,20 @@
         return 0
 
     lax.fori_loop(1, chips, close_far, 0)
+    hop.wait_send()
+    for q in range(pieces):
+        early_copy(q).wait_send()
     hub_copy(me, sibling, 0).wait_send()
 
     @pl.when(me > 0)
     def _():
         down.wait_send()
+        early_down.wait_send()
 
     @pl.when(me < n - 1)
     def _():
         up.wait_send()
+        early_up.wait_send()
 
 
 def shards(
@@ -362,45 +509,52 @@
     limit = jnp.concatenate([seq, jnp.full((blocks,), total, i32)])
     same = (row_of[None, :] == target[:, None]) & (seq[None, :] < limit[:, None])
     chain = jnp.max(jnp.where(same, seq[None, :] + 1, 0), axis=1)
-    meta = jnp.concatenate(
-        [
-            local_cols[0] - (blocks - REACH),
-            hub_panels[0],
-            chain,
-            hub_ids - lax.axis_index("dom") * rows,
-        ]
-    )
 
     vmem = pl.BlockSpec(memory_space=pltpu.VMEM)
     smem = pl.BlockSpec(memory_space=pltpu.SMEM)
     anym = pl.BlockSpec(memory_space=pl.ANY)
     dma = pltpu.SemaphoreType.DMA
     flops = 6 * BLK * BLK * half * total + 6 * rows * 2 * half * half
-    return pl.pallas_call(
+    part = half // 2
+    halo = REACH * BLK
+    pieces = rows // halo
+    normed = pl.pallas_call(
         functools.partial(kernel, n, rows, half, hd, slots, tiles, chunk),
         out_shape=jax.ShapeDtypeStruct((rows, half), F32),
-        in_specs=[vmem, vmem, vmem, smem, anym, anym, vmem, vmem, vmem],
+        in_specs=[anym, vmem, vmem, smem, smem, smem, smem, anym, anym, vmem, vmem],
         out_specs=anym,
         scratch_shapes=[
             pltpu.VMEM((rows, half), F32),
             pltpu.VMEM((REACH * BLK, half), F32),
             pltpu.VMEM((REACH * BLK, half), F32),
-            pltpu.VMEM((n * hd, half), F32),
+            pltpu.VMEM((rows, part), F32),
+            pltpu.VMEM((rows, part), F32),
+            pltpu.VMEM((halo, part), F32),
+            pltpu.VMEM((halo, part), F32),
+            pltpu.VMEM((hd, part), F32),
+            pltpu.VMEM((hd, part), F32),
+            pltpu.VMEM((n * hd, half + part), F32),
             pltpu.VMEM((blocks + 2 * REACH, 3 * BLK, half), BF16),
             pltpu.VMEM((n * hd // BLK, 3 * BLK, half), BF16),
             pltpu.VMEM((total, BLK, BLK), F32),
             pltpu.VMEM((total + 1, BLK, half), F32),
             pltpu.VMEM((rows, half), F32),
+            pltpu.VMEM((rows, part), F32),
+            pltpu.VMEM((rows, part), F32),
             pltpu.VMEM((rows, half), F32),
-            pltpu.VMEM((rows, half), F32),
-            pltpu.VMEM((2, 3 * half, half), BF16),
+            pltpu.VMEM((6 * half, half), BF16),
             pltpu.VMEM((chunks, 8, chunk), F32),
             pltpu.VMEM((chunks, 8, chunk), F32),
             dma((2,)),
+            dma((pieces,)),
+            dma((pieces,)),
+            dma((pieces,)),
+            dma((1,)),
+            dma((1,)),
             dma((n,)),
             dma((n,)),
-            dma((2,)),
-            dma((2,)),
+            dma((4,)),
+            dma((4,)),
             dma((chunks,)),
             dma((chunks,)),
             dma((chunks,)),
@@ -415,13 +569,16 @@
         features,
         infill_mask.reshape(blocks, BLK),
         mask_token[None, :],
-        meta,
+        local_cols,
+        hub_panels,
+        hub_ids,
+        chain,
         local_tiles[0],
         hub_tiles[0],
         mix_weight,
         mix_bias[None, :],
-        norm_gain[None, :],
     )
+    return normed * norm_gain[None, :]
 
 
 def solution(mesh):

time: 94.3 us -> 75.6 us (0.80)
  Pallas kernels: 84.5 us -> 68.1 us
  local copies, waits for them, and re-layouts: 3.05 us -> 0.01 us
  other arithmetic: 5.61 us -> 6.59 us
    pallas_call x1, Pallas kernels: 84.5 us -> 68.1 us  [shards(): pl.pallas_call(functools.partial(kernel, n, rows, half, hd, slots, tiles,...]
    mul x0 -> x1, other arithmetic: none -> 3.05 us  [shards(): return normed * norm_gain[None, :]]
    unnamed x1 -> x2, local copies, waits for them, and re-layouts: 3.05 us -> 0.01 us
    sub x2 -> x0, other arithmetic: 1.31 us -> none  [the longest x1 0.66 us: shards(): hub_ids - lax.axis_index('dom') * rows]
    concatenate x1 -> x0, other arithmetic: 1.31 us -> none  [shards(): jnp.concatenate([local_cols[0] - (blocks - REACH), hub_panels[0], chain,...]
where the time goes in v2:
time: 75.6 us; the launch traced here: 75.4 us
  Pallas kernels  68.1 us (90%)
  other arithmetic  6.59 us (9%)
    pallas_call x1, Pallas kernels, shards(): pl.pallas_call(functools.partial(kernel, n, rows, half, hd, slots, tiles,...  68.1 us
    mul x1, other arithmetic, shards(): return normed * norm_gain[None, :]  3.05 us

profile of v2, /device:TPU:0, one launch (start us, length us, event | category | flops | bytes accessed | tf_op | source)
XLA Modules:
  0.0 75.4 jit_solution(10253311594308160379)
XLA Ops:
  0.7 0.7 compare_select_fusion
  1.3 0.7 pad_add_fusion
  2.0 0.7 pad_add_fusion.1
  2.8 1.4 %select_reduce_fusion.chain_ref = s32[144]{0:T(256)} fusion(s32[128]{0:T(128)S(1)} %get-tuple-element.6, s32[144]{0:T(256)} %constant.2.clone.1, s32[128]{0:T(128)S(1)} %get-tuple-element.5, s32[144]{0:T(256)S(1)} %pad_add_fusion), kind=kLoop, calls=%fused_computation.1 | loop fusion | flops 92016 | bytes 2752 | tf_op jit(solution)/shard_map/reduce_max | solution.py:511
  4.2 0.0 copy-start
  4.2 68.1 %shard_map.136 = f32[2048,256]{1,0:T(8,128)} custom-call(f32[2048,256]{1,0:T(8,128)} %feat_ref.1, s32[16,128]{1,0:T(8,128)} %bitcast.14, f32[1,256]{1,0:T(1,128)} %bitcast.15, s32[1,64]{1,0:T(1,128)} %cols_ref.1, s32[1,64]{1,0:T(1,128)} %panels_ref.1, s32[32]{0:T(128)} %ids_ref.1, s32[144]{0:T(256)} %select_reduce_fusion.chain_ref, ...), custom_call_target="tpu_custom_call" | custom-call | flops 4831838208 | bytes 13631488 | tf_op jit(solution)/shard_map/pallas_call | solution.py:521
  72.3 0.0 copy-done
  72.3 3.0 %broadcast_multiply_fusion = f32[2048,256]{1,0:T(8,128)} fusion(f32[2048,256]{1,0:T(8,128)} %shard_map.136, f32[256]{0:T(256)S(1)} %copy-done), kind=kLoop, calls=%fused_computation | loop fusion | flops 524288 | bytes 4195328 | tf_op jit(solution)/shard_map/mul | solution.py:581
  (1 shorter events, 0.0 us)
Async XLA Ops:
  4.2 68.1 %copy-start = (f32[256]{0:T(256)S(1)}, f32[256]{0:T(256)}, u32[]{:S(2)}) copy-start(f32[256]{0:T(256)} %param.27) | copy-start | bytes 3076

commit v3 on v2

--- a/solution.py
+++ b/solution.py
@@ -59,6 +59,7 @@
     hub_out,
     hub_in,
     hubs,
+    hubs_early,
     ext_b,
     hub_b,
     tl,
@@ -78,6 +79,8 @@
     hop_recv,
     hub_send,
     hub_recv,
+    hub_early_send,
+    hub_early_recv,
     halo_send,
     halo_recv,
     agg_send,
@@ -142,13 +145,63 @@
 
     def pick(i, _):
         got = fil[pl.ds(jnp.maximum(ids_ref[i] - first, 0), 1), :]
-        hubs[pl.ds(base + i, 1), 0:half] = got
+        hubs[pl.ds(base + i, 1), :] = got
         hub_out[pl.ds(i, 1), :] = got[:, part:]
         return 0
 
     lax.fori_loop(0, hd, pick, 0)
 
     pl.semaphore_wait(barrier, n)
+
+    def copies_of(buffer, sends, recvs):
+        def hub_copy(owner, target, sem_at):
+            at = pl.ds(pl.multiple_of(owner * hd, hd), hd)
+            return pltpu.make_async_remote_copy(
+                src_ref=buffer.at[at],
+                dst_ref=buffer.at[at],
+                send_sem=sends.at[sem_at],
+                recv_sem=recvs.at[owner],
+                device_id={"dom": target},
+            )
+
+        return hub_copy
+
+    def send_own(hub_copy):
+        def send_far(j, _):
+            hub_copy(me, lax.rem(me + 2 * j, n), j).start()
+            return 0
+
+        lax.fori_loop(1, chips, send_far, 0)
+        hub_copy(me, sibling, 0).start()
+
+    def pass_on(hub_copy):
+        def forward(j, _):
+            owner = lax.rem(me + n - 2 * j, n)
+            hub_copy(owner, sibling, 0).wait_recv()
+            hub_copy(owner, sibling, chips + j).start()
+            return 0
+
+        lax.fori_loop(1, chips, forward, 0)
+
+    def await_sibling(hub_copy):
+        def arrive(j, _):
+            hub_copy(lax.rem(sibling + n - 2 * j, n), sibling, 0).wait_recv()
+            return 0
+
+        lax.fori_loop(0, chips, arrive, 0)
+
+    def close_sends(hub_copy):
+        def close_far(j, _):
+            hub_copy(me, sibling, j).wait_send()
+            hub_copy(me, sibling, chips + j).wait_send()
+            return 0
+
+        lax.fori_loop(1, chips, close_far, 0)
+        hub_copy(me, sibling, 0).wait_send()
+
+    main_copy = copies_of(hubs, hub_send, hub_recv)
+    side_copy = copies_of(hubs_early, hub_early_send, hub_early_recv)
+    send_own(main_copy)
 
     hop = pltpu.make_async_remote_copy(
         src_ref=hub_out,
@@ -172,26 +225,6 @@
     order = [0, pieces - 1] + list(range(1, pieces - 1))
     for q in order:
         early_copy(q).start()
-
-    def hub_copy(owner, target, sem_at):
-        at = pl.ds(pl.multiple_of(owner * hd, hd), hd)
-        return pltpu.make_async_remote_copy(
-            src_ref=hubs.at[at],
-            dst_ref=hubs.at[at],
-            send_sem=hub_send.at[sem_at],
-            recv_sem=hub_recv.at[owner],
-            device_id={"dom": target},
-        )
-
-    hop.wait_recv()
-    hubs[pl.ds(base, hd), half:] = hub_in[...]
-
-    def send_far(j, _):
-        hub_copy(me, lax.rem(me + 2 * j, n), j).start()
-        return 0
-
-    lax.fori_loop(1, chips, send_far, 0)
-    hub_copy(me, sibling, 0).start()
 
     down = pltpu.make_async_remote_copy(
         src_ref=fil.at[pl.ds(0, halo)],
@@ -238,22 +271,11 @@
     w_b[pl.ds(3 * half + 3 * part, 3 * part), :] = right_form(w_far[:part, :])
     sums[0] = jnp.zeros((BLK, half), F32)
 
-    def forward(j, _):
-        owner = lax.rem(me + n - 2 * j, n)
-        hub_copy(owner, sibling, 0).wait_recv()
-        hub_copy(owner, sibling, chips + j).start()
-        return 0
-
-    lax.fori_loop(1, chips, forward, 0)
-
-    def arrive(j, _):
-        hub_copy(lax.rem(sibling + n - 2 * j, n), sibling, 0).wait_recv()
-        return 0
-
-    lax.fori_loop(0, chips, arrive, 0)
+    pass_on(main_copy)
+    await_sibling(main_copy)
 
     def panel_form(p, _):
-        hub_b[p] = right_form(hubs[pl.ds(pl.multiple_of(p * BLK, BLK), BLK), 0:half])
+        hub_b[p] = right_form(hubs[pl.ds(pl.multiple_of(p * BLK, BLK), BLK), :])
         return 0
 
     lax.fori_loop(0, panels, panel_form, 0)
@@ -261,7 +283,7 @@
 
     last_at = slots + tiles
     shift = blocks - REACH
-    group = 4
+    group = 16
 
     def hub_products(g, _):
         for u in range(group):
@@ -272,6 +294,9 @@
 
     lax.fori_loop(0, slots // group, hub_products, 0)
 
+    hop.wait_recv()
+    hubs_early[pl.ds(base, hd), :] = hub_in[...]
+    send_own(side_copy)
     early_copy(0).wait_recv()
     early_copy(pieces - 1).wait_recv()
 
@@ -351,8 +376,41 @@
 
     lax.fori_loop(0, chunks, send_chunk, 0)
 
+    pass_on(side_copy)
+
+    for q in range(1, pieces - 1):
+        early_copy(q).wait_recv()
+
+    def own_early(b, _):
+        ext_b[REACH + b, :, 0:part] = right_form(early_in[pl.ds(pl.multiple_of(b * BLK, BLK), BLK), :])
+        return 0
+
+    lax.fori_loop(0, blocks, own_early, 0)
+
+    @pl.when(me > 0)
+    def _():
+        early_up.wait_recv()
+
+    @pl.when(me == 0)
+    def _():
+        early_lo[...] = jnp.zeros((halo, part), F32)
+
+    @pl.when(me < n - 1)
+    def _():
+        early_down.wait_recv()
+
+    @pl.when(me == n - 1)
+    def _():
+        early_hi[...] = jnp.zeros((halo, part), F32)
+
+    for b in range(REACH):
+        ext_b[b, :, 0:part] = right_form(early_lo[pl.ds(b * BLK, BLK), :])
+        ext_b[REACH + blocks + b, :, 0:part] = right_form(early_hi[pl.ds(b * BLK, BLK), :])
+
+    await_sibling(side_copy)
+
     def hub_early(p, _):
-        hub_b[p, :, 0:part] = right_form(hubs[pl.ds(pl.multiple_of(p * BLK, BLK), BLK), half:])
+        hub_b[p, :, 0:part] = right_form(hubs_early[pl.ds(pl.multiple_of(p * BLK, BLK), BLK), :])
         return 0
 
     lax.fori_loop(0, panels, hub_early, 0)
@@ -366,35 +424,6 @@
         return 0
 
     lax.fori_loop(0, slots // group, hub_products_early, 0)
-
-    for q in range(1, pieces - 1):
-        early_copy(q).wait_recv()
-
-    def own_early(b, _):
-        ext_b[REACH + b, :, 0:part] = right_form(early_in[pl.ds(pl.multiple_of(b * BLK, BLK), BLK), :])
-        return 0
-
-    lax.fori_loop(0, blocks, own_early, 0)
-
-    @pl.when(me > 0)
-    def _():
-        early_up.wait_recv()
-
-    @pl.when(me == 0)
-    def _():
-        early_lo[...] = jnp.zeros((halo, part), F32)
-
-    @pl.when(me < n - 1)
-    def _():
-        early_down.wait_recv()
-
-    @pl.when(me == n - 1)
-    def _():
-        early_hi[...] = jnp.zeros((halo, part), F32)
-
-    for b in range(REACH):
-        ext_b[b, :, 0:part] = right_form(early_lo[pl.ds(b * BLK, BLK), :])
-        ext_b[REACH + blocks + b, :, 0:part] = right_form(early_hi[pl.ds(b * BLK, BLK), :])
 
     def loc_products_early(g, _):
         for u in range(group):
@@ -453,16 +482,11 @@
 
     lax.fori_loop(0, chunks, close, 0)
 
-    def close_far(j, _):
-        hub_copy(me, sibling, j).wait_send()
-        hub_copy(me, sibling, chips + j).wait_send()
-        return 0
-
-    lax.fori_loop(1, chips, close_far, 0)
+    close_sends(main_copy)
+    close_sends(side_copy)
     hop.wait_send()
     for q in range(pieces):
         early_copy(q).wait_send()
-    hub_copy(me, sibling, 0).wait_send()
 
     @pl.when(me > 0)
     def _():
@@ -533,7 +557,8 @@
             pltpu.VMEM((halo, part), F32),
             pltpu.VMEM((hd, part), F32),
             pltpu.VMEM((hd, part), F32),
-            pltpu.VMEM((n * hd, half + part), F32),
+            pltpu.VMEM((n * hd, half), F32),
+            pltpu.VMEM((n * hd, part), F32),
             pltpu.VMEM((blocks + 2 * REACH, 3 * BLK, half), BF16),
             pltpu.VMEM((n * hd // BLK, 3 * BLK, half), BF16),
             pltpu.VMEM((total, BLK, BLK), F32),
@@ -551,6 +576,8 @@
             dma((pieces,)),
             dma((1,)),
             dma((1,)),
+            dma((n,)),
+            dma((n,)),
             dma((n,)),
             dma((n,)),
             dma((4,)),

time: 75.6 us -> 76.8 us (1.016)
  Pallas kernels: 68.1 us -> 69.3 us
    pallas_call x1, Pallas kernels: 68.1 us -> 69.3 us  [shards(): pl.pallas_call(functools.partial(kernel, n, rows, half, hd, slots, tiles,...]
where the time goes in v3:
time: 76.8 us; the launch traced here: 76.5 us
  Pallas kernels  69.3 us (90%)
  other arithmetic  6.59 us (9%)
    pallas_call x1, Pallas kernels, shards(): pl.pallas_call(functools.partial(kernel, n, rows, half, hd, slots, tiles,...  69.3 us
    mul x1, other arithmetic, shards(): return normed * norm_gain[None, :]  3.05 us

profile of v3, /device:TPU:0, one launch (start us, length us, event | category | flops | bytes accessed | tf_op | source)
XLA Modules:
  0.0 76.5 jit_solution(2480979365918929168)
XLA Ops:
  0.7 0.7 compare_select_fusion
  1.3 0.7 pad_add_fusion
  2.0 0.7 pad_add_fusion.1
  2.8 1.4 %select_reduce_fusion.chain_ref = s32[144]{0:T(256)} fusion(s32[128]{0:T(128)S(1)} %get-tuple-element.6, s32[144]{0:T(256)} %constant.2.clone.1, s32[128]{0:T(128)S(1)} %get-tuple-element.5, s32[144]{0:T(256)S(1)} %pad_add_fusion), kind=kLoop, calls=%fused_computation.1 | loop fusion | flops 92016 | bytes 2752 | tf_op jit(solution)/shard_map/reduce_max | solution.py:535
  4.2 0.0 copy-start
  4.2 69.3 %shard_map.136 = f32[2048,256]{1,0:T(8,128)} custom-call(f32[2048,256]{1,0:T(8,128)} %feat_ref.1, s32[16,128]{1,0:T(8,128)} %bitcast.14, f32[1,256]{1,0:T(1,128)} %bitcast.15, s32[1,64]{1,0:T(1,128)} %cols_ref.1, s32[1,64]{1,0:T(1,128)} %panels_ref.1, s32[32]{0:T(128)} %ids_ref.1, s32[144]{0:T(256)} %select_reduce_fusion.chain_ref, ...), custom_call_target="tpu_custom_call" | custom-call | flops 4831838208 | bytes 13631488 | tf_op jit(solution)/shard_map/pallas_call | solution.py:545
  73.5 0.0 copy-done
  73.5 3.0 %broadcast_multiply_fusion = f32[2048,256]{1,0:T(8,128)} fusion(f32[2048,256]{1,0:T(8,128)} %shard_map.136, f32[256]{0:T(256)S(1)} %copy-done), kind=kLoop, calls=%fused_computation | loop fusion | flops 524288 | bytes 4195328 | tf_op jit(solution)/shard_map/mul | solution.py:608
  (1 shorter events, 0.0 us)
Async XLA Ops:
  4.2 69.3 %copy-start = (f32[256]{0:T(256)S(1)}, f32[256]{0:T(256)}, u32[]{:S(2)}) copy-start(f32[256]{0:T(256)} %param.27) | copy-start | bytes 3076
